TPU v7x, 32 devices: a whole 2x2x4 slice. The times are simulated.
32 devices in a mesh: gx: 4 (over y, x), gy: 8 (over z, core).
Axes of the slice: x: 2, y: 2, z: 4, core: 2. Of those that a mesh axis runs over, the one named last changes fastest.
Arguments:
- vectors: float32 [16, 13, 16, 1024], P(None, None, 'gx', 'gy'), may hold values from -6 to 6
- features: bfloat16 [128, 16, 1024], P(None, 'gx', 'gy'), may hold values from -6 to 6
- gains: float32 [25, 128], replicated, may hold values from 0.25 to 1.5
- edge_weight: bfloat16 [128, 169], replicated, may hold values from -0.01953125 to 0.01953125
- energies: float32 [13, 3], replicated, may hold values from -0.5 to 0.5
- neighbours: int32 [12, 16, 1024], P(None, 'gx', 'gy'), may hold values from -1 to 24, as said below
- species: int32 [16, 1024], P('gx', 'gy'), may hold values from 0 to 2
Outputs:
- evolved: float32 [16, 13, 16, 1024], P(None, None, 'gx', 'gy')
Inputs may be any that keep to these rules, and one draw needn't show every extreme that they name: `neighbours`: code c names the atom c // 5 - 2 rows and c % 5 - 2 columns away on the periodic slab; 12 never appears; one atom's codes are distinct; -1 marks an empty slot.
All inputs are finite; a program needn't handle non-finite values.
Results may differ from a plain program's by a relative error of at most 0.009.
Values may be sent and summed in bfloat16 or wider, within the bound.
A program may use at most 64 MiB of HBM per device.

v0:
```python
import functools

import jax
import jax.numpy as jnp
from jax import lax
from jax.experimental import pallas as pl
from jax.experimental.pallas import tpu as pltpu
from jax.sharding import PartitionSpec as P

STEPS = 4
CODES = 25
LANES = 128
MESH = pl.DeviceIdType.MESH
ROUTES = ((-1, 0), (1, 0), (0, -1), (-1, -1), (1, -1), (0, 1), (-1, 1), (1, 1))


def neighbour_id(offset):
    place = {}
    for name, step in zip(("gx", "gy"), offset):
        count = lax.axis_size(name)
        place[name] = lax.rem(lax.axis_index(name) + step + count, count)
    return place


def lane_ids(rows, width):
    return lax.broadcasted_iota(jnp.int32, (rows, width), 1)


def exchange(sources, targets, send_sem, recv_sem, which):
    copies = []
    for route, offset in enumerate(ROUTES):
        copy = pltpu.make_async_remote_copy(
            src_ref=sources[route],
            dst_ref=targets[route],
            send_sem=send_sem.at[which, route],
            recv_sem=recv_sem.at[which, route],
            device_id=neighbour_id(offset),
            device_id_type=MESH,
        )
        copy.start()
        copies.append(copy)
    return copies


def shifts(centre, left, right):
    rows, width = centre.shape
    ids = lane_ids(rows, LANES)
    first = centre[:, :LANES]
    last = centre[:, width - LANES :]

    def before(count):
        edge = jnp.where(ids >= LANES - count, left, last)
        if width > LANES:
            edge = jnp.concatenate([centre[:, : width - LANES], edge], axis=1)
        return pltpu.roll(edge, count, 1)

    def after(count):
        edge = jnp.where(ids < count, right, first)
        if width > LANES:
            edge = jnp.concatenate([edge, centre[:, LANES:]], axis=1)
        return pltpu.roll(edge, width - count, 1)

    return [before(2), before(1), centre, after(1), after(2)]


def kernel(
    orbits,
    groups,
    vec_ref,
    feat_ref,
    gain_ref,
    weight_ref,
    onsite_ref,
    near_ref,
    out_ref,
    blk,
    moved,
    state,
    feat_moved,
    mm,
    tmp,
    feat_cols,
    feat_rows_in,
    feat_cols_in,
    rows_out,
    cols_out,
    rows_in,
    cols_in,
    side,
    send_sem,
    recv_sem,
):
    width = vec_ref.shape[2]
    chunks = width // LANES
    fields = groups * orbits
    entries = orbits * orbits
    f32, bf16 = jnp.float32, jnp.bfloat16

    barrier = pltpu.get_barrier_semaphore()
    for offset in ROUTES:
        pl.semaphore_signal(barrier, inc=1, device_id=neighbour_id(offset), device_id_type=MESH)
    pl.semaphore_wait(barrier, len(ROUTES))

    ids = lane_ids(feat_ref.shape[1], LANES)
    low_cols = jnp.zeros(ids.shape, f32)
    high_cols = jnp.zeros(ids.shape, f32)
    for row in range(4):
        held = (ids >= 2 * row) & (ids < 2 * row + 2)
        low = feat_ref[row, :, :LANES].astype(f32)
        high = feat_ref[row, :, width - LANES :].astype(f32)
        low_cols = jnp.where(held, pltpu.roll(low, 2 * row, 1) if row else low, low_cols)
        high_cols = jnp.where(held, pltpu.roll(high, 2 * row + 2, 1), high_cols)
    feat_cols[0] = low_cols.astype(bf16)
    feat_cols[1] = high_cols.astype(bf16)
    feat_copies = exchange(
        [feat_ref.at[pl.ds(0, 2)], feat_ref.at[pl.ds(2, 2)]]
        + [feat_cols.at[0]] * 3
        + [feat_cols.at[1]] * 3,
        [feat_rows_in.at[0], feat_rows_in.at[1]] + [feat_cols_in.at[k] for k in range(6)],
        send_sem,
        recv_sem,
        0,
    )

    def send_state(current, step):
        ids16 = lane_ids(16, LANES)

        def pack(pair, cols):
            low_cols, high_cols = cols
            a = current[2 * pair]
            b = current[2 * pair + 1]
            rows_out[step, 0, pair] = jnp.concatenate([a[0:8], b[0:8]], axis=0).astype(bf16)
            rows_out[step, 1, pair] = jnp.concatenate([a[8:16], b[8:16]], axis=0).astype(bf16)
            for half, tile in enumerate((a, b)):
                spot = 4 * pair + 2 * half
                held = (ids16 >= spot) & (ids16 < spot + 2)
                low_cols = jnp.where(held, pltpu.roll(tile[:, :LANES], spot, 1), low_cols)
                high_cols = jnp.where(
                    held, pltpu.roll(tile[:, width - LANES :], lax.rem(spot + 2, LANES), 1), high_cols
                )
            return low_cols, high_cols

        zero = jnp.zeros((16, LANES), f32)
        low_cols, high_cols = lax.fori_loop(0, fields // 2, pack, (zero, zero))
        cols_out[step, 0] = low_cols.astype(bf16)
        cols_out[step, 1] = high_cols.astype(bf16)
        return exchange(
            [rows_out.at[step, 0], rows_out.at[step, 1]]
            + [cols_out.at[step, 0]] * 3
            + [cols_out.at[step, 1]] * 3,
            [rows_in.at[step, 0], rows_in.at[step, 1]] + [cols_in.at[step, k] for k in range(6)],
            send_sem,
            recv_sem,
            step + 1,
        )

    copies = send_state(vec_ref, 0)

    for copy in feat_copies:
        copy.wait()
    for row in range(8):
        if row < 2:
            tile, which, spot = feat_rows_in[1, row], 2, row + 2
        elif row < 6:
            tile, which, spot = feat_ref[row - 2], 0, row - 2
        else:
            tile, which, spot = feat_rows_in[0, row - 6], 1, row - 6
        right = pltpu.roll(feat_cols_in[which].astype(f32), (LANES - 2 * spot) % LANES, 1) if spot else feat_cols_in[which].astype(f32)
        left = pltpu.roll(feat_cols_in[3 + which].astype(f32), LANES - 2 - 2 * spot, 1)
        for shift, moved_tile in enumerate(shifts(tile.astype(f32), left, right)):
            feat_moved[shift, row] = moved_tile.astype(bf16)

    sub8 = lax.broadcasted_iota(jnp.int32, (8, width), 0) < 4

    def build(code, carry):
        code_x = code // 5
        code_y = code - 5 * code_x
        present = jnp.where(code == 12, jnp.ones((4, width), f32), jnp.zeros((4, width), f32))
        for slot in range(near_ref.shape[0]):
            present = jnp.where(near_ref[slot] == code, 1.0, present)
        turned = pltpu.roll(gain_ref[...], lax.rem(LANES - code, LANES), 1)
        gain = jnp.broadcast_to(turned[:, 0:1], (turned.shape[0], width))
        for row in range(4):
            own = feat_ref[row].astype(f32)
            peer = feat_moved[code_y, code_x + row].astype(f32)
            edge = own * peer * gain * present[row : row + 1]
            mm[row] = jnp.dot(weight_ref[...], edge.astype(bf16), preferred_element_type=f32)

        @pl.when(code == 12)
        def _():
            for row in range(4):
                for orbit in range(orbits):
                    spot = orbit * (orbits + 1)
                    mm[row, pl.ds(spot, 1), :] += onsite_ref[row, pl.ds(orbit, 1), :]

        def expand(orbit, inner):
            for other in range(orbits):
                spot = orbit * orbits + other
                lines = [
                    jnp.broadcast_to(mm[row, pl.ds(spot, 1), :], (8, width)) for row in range(4)
                ]
                top = jnp.where(sub8, lines[0], lines[1])
                low = jnp.where(sub8, lines[2], lines[3])
                blk[code * entries + spot] = jnp.concatenate([top, low], axis=0).astype(bf16)
            return inner

        lax.fori_loop(0, orbits, expand, 0)
        return carry

    lax.fori_loop(0, CODES, build, 0)

    tiles = []
    start = 0
    while start < orbits:
        size = 4 if (orbits - start) % 3 else 3
        tiles.append((start, min(size, orbits - start)))
        start += size

    for step in range(STEPS):
        current = vec_ref if step == 0 else state.at[(step - 1) % 2]
        for copy in copies:
            copy.wait()
        for which, base in enumerate((3, 0)):
            side[which, 0:8] = cols_in[step, base + 2].astype(f32)[8:16]
            side[which, 8:24] = cols_in[step, base].astype(f32)
            side[which, 24:32] = cols_in[step, base + 1].astype(f32)[0:8]

        def spread(pair, carry):
            above = rows_in[step, 1, pair].astype(f32)
            below = rows_in[step, 0, pair].astype(f32)
            for half in range(2):
                field = 2 * pair + half
                spot = 2 * field
                centre = jnp.concatenate(
                    [above[8 * half : 8 * half + 8], current[field], below[8 * half : 8 * half + 8]],
                    axis=0,
                )
                left = pltpu.roll(side[0], lax.rem(LANES - 2 - spot + LANES, LANES), 1)
                right = pltpu.roll(side[1], lax.rem(LANES - spot, LANES), 1)
                for shift, tile in enumerate(shifts(centre, left, right)):
                    for chunk in range(chunks):
                        cols = slice(chunk * LANES, (chunk + 1) * LANES)
                        tmp[half, shift, chunk] = tile[:, cols]
                        for lift in range(5):
                            moved[lift * 5 + shift, field, :, cols] = tmp[
                                half, shift, chunk, 4 * lift : 4 * lift + 16
                            ].astype(bf16)
            return carry

        lax.fori_loop(0, fields // 2, spread, 0)

        target = out_ref if step == STEPS - 1 else state.at[step % 2]
        previous = vec_ref if step == 1 else state.at[step % 2]
        for chunk in range(chunks):
            cols = slice(chunk * LANES, (chunk + 1) * LANES)
            for start, size in tiles:

                def gather(code, sums):
                    parts = [[None, None] for _ in range(size * groups)]
                    for other in range(orbits):
                        chain = 0 if other < 7 else 1
                        fields_in = [moved[code, g * orbits + other, :, cols] for g in range(groups)]
                        for k in range(size):
                            entry = blk[code * entries + (start + k) * orbits + other, :, cols]
                            for g in range(groups):
                                part = parts[k * groups + g]
                                term = entry * fields_in[g]
                                part[chain] = term if part[chain] is None else part[chain] + term
                    return tuple(
                        total + (part[0] + part[1]).astype(f32) for total, part in zip(sums, parts)
                    )

                zero = jnp.zeros((16, LANES), f32)
                sums = lax.fori_loop(0, CODES, gather, (zero,) * (size * groups))
                for k in range(size):
                    for g in range(groups):
                        field = g * orbits + start + k
                        value = sums[k * groups + g]
                        if step:
                            value = 2.0 * value - previous[field, :, cols]
                        target[field, :, cols] = value
        if step < STEPS - 1:
            copies = send_state(target, step + 1)


def body(vectors, features, gains, edge_weight, energies, neighbours, species):
    count, orbits, rows, width = vectors.shape
    groups = count // 4
    channels = features.shape[0]
    entries = orbits * orbits
    padded = -(-entries // 16) * 16
    fields = groups * orbits
    f32, bf16 = jnp.float32, jnp.bfloat16
    vec = vectors.reshape(groups, 4, orbits, rows, width).transpose(0, 2, 3, 1, 4)
    vec = vec.reshape(fields, rows * 4, width)
    feat = features.transpose(1, 0, 2)
    gain = jnp.pad(gains.T, ((0, 0), (0, LANES - gains.shape[0])))
    weight = jnp.pad(edge_weight.T, ((0, padded - entries), (0, 0)))
    onsite = jnp.zeros((rows, orbits, width), f32)
    for kind in range(energies.shape[1]):
        onsite = jnp.where(species[:, None] == kind, energies[:, kind][None, :, None], onsite)
    vmem = pl.BlockSpec(memory_space=pltpu.VMEM)
    out = pl.pallas_call(
        functools.partial(kernel, orbits, groups),
        out_shape=jax.ShapeDtypeStruct(vec.shape, f32),
        in_specs=[vmem] * 6,
        out_specs=vmem,
        scratch_shapes=[
            pltpu.VMEM((CODES * entries, 16, width), bf16),
            pltpu.VMEM((CODES, fields, 16, width), bf16),
            pltpu.VMEM((2, fields, 16, width), f32),
            pltpu.VMEM((5, rows + 4, channels, width), bf16),
            pltpu.VMEM((rows, padded, width), f32),
            pltpu.VMEM((2, 5, width // LANES, 32, LANES), f32),
            pltpu.VMEM((2, channels, LANES), bf16),
            pltpu.VMEM((2, 2, channels, width), bf16),
            pltpu.VMEM((6, channels, LANES), bf16),
            pltpu.VMEM((STEPS, 2, fields // 2, 16, width), bf16),
            pltpu.VMEM((STEPS, 2, 16, LANES), bf16),
            pltpu.VMEM((STEPS, 2, fields // 2, 16, width), bf16),
            pltpu.VMEM((STEPS, 6, 16, LANES), bf16),
            pltpu.VMEM((2, 32, LANES), f32),
            pltpu.SemaphoreType.DMA((STEPS + 1, len(ROUTES))),
            pltpu.SemaphoreType.DMA((STEPS + 1, len(ROUTES))),
        ],
        compiler_params=pltpu.CompilerParams(
            collective_id=0, has_side_effects=True, vmem_limit_bytes=62 * 1024 * 1024
        ),
        cost_estimate=pl.CostEstimate(
            flops=STEPS * 2 * CODES * entries * count * rows * width,
            bytes_accessed=4 * 1024 * 1024,
            transcendentals=0,
        ),
    )(vec, feat, gain, weight, onsite, neighbours)
    out = out.reshape(groups, orbits, rows, 4, width).transpose(0, 3, 1, 2, 4)
    return out.reshape(vectors.shape)


def solution(mesh):
    return jax.shard_map(
        body,
        mesh=mesh,
        in_specs=(
            P(None, None, "gx", "gy"),
            P(None, "gx", "gy"),
            P(),
            P(),
            P(),
            P(None, "gx", "gy"),
            P("gx", "gy"),
        ),
        out_specs=P(None, None, "gx", "gy"),
        check_vma=False,
    )
```

profile of v0, /device:TPU:0, one launch (start us, length us, event | category | flops | bytes accessed | tf_op | source)
XLA Modules:
  0.0 129.9 jit_solution(15628064181539816079)
XLA Ops:
  0.0 0.0 copy-start.2
  0.0 0.0 copy-start.1
  0.0 0.0 copy-start
  0.0 0.7 copy-done.2
  0.7 0.7 broadcast_compare_fusion.2
  1.4 0.7 select_select_fusion.onsite_ref
  2.0 0.0 copy-done.1
  2.0 0.6 pad.9.weight_ref
  2.7 0.8 copy.10
  3.5 0.6 pad.8.gain_ref
  4.1 1.6 %copy.13 = bf16[128,4,128]{2,0,1:T(8,128)(2,1)} copy(bf16[128,4,128]{2,1,0:T(4,128)(2,1)} %param.8) | data formatting | bytes 262144 | tf_op args[1]
  5.7 0.0 copy-done
  5.7 0.9 copy.8
  6.6 121.4 %shard_map.73 = f32[52,16,128]{2,1,0:T(8,128)} custom-call(f32[52,16,128]{2,1,0:T(8,128)} %bitcast.20, bf16[4,128,128]{2,1,0:T(8,128)(2,1)} %bitcast.21, f32[128,128]{1,0:T(8,128)} %pad.8.gain_ref, bf16[176,128]{1,0:T(8,128)(2,1)} %pad.9.weight_ref, f32[4,13,128]{2,1,0:T(8,128)} %select_select_fusion.onsite_ref, s32[12,4,128]{2,1,0:T(4,128)} %near_ref.1), custom_call_target="tpu_custom_call" | custom-call | flops 276889600 | bytes 4194304 | tf_op jit(solution)/shard_map/pallas_call | solution.py:303
  128.0 1.9 %copy.11 = f32[4,4,13,4,128]{4,3,2,1,0:T(4,128)} copy(f32[4,4,13,4,128]{4,1,3,2,0:T(4,128)} %bitcast.19) | data formatting | bytes 851968 | tf_op jit(solution)/shard_map/transpose | solution.py:335
  (1 shorter events, 0.0 us)
Async XLA Ops:
  0.0 0.7 copy-start.2
  0.0 2.0 %copy-start.1 = (bf16[128,169]{0,1:T(8,128)(2,1)S(1)}, bf16[128,169]{0,1:T(8,128)(2,1)}, u32[]{:S(2)}) copy-start(bf16[128,169]{0,1:T(8,128)(2,1)} %param.10) | copy-start | bytes 129796
  0.0 5.7 %copy-start = (f32[16,13,4,128]{3,2,1,0:T(4,128)S(1)}, f32[16,13,4,128]{3,2,1,0:T(4,128)}, u32[]{:S(2)}) copy-start(f32[16,13,4,128]{3,2,1,0:T(4,128)} %param.7) | copy-start | bytes 1277956
where the time goes:
time: 130 us
  Pallas kernels  121 us (93%)
  local copies, waits for them, and re-layouts  7.08 us (5%)
  other arithmetic  1.36 us (1%)
    pallas_call x1, Pallas kernels, body(): pl.pallas_call(functools.partial(kernel, orbits, groups), out_shape=jax.S...  121 us
    unnamed x8, local copies, waits for them, and re-layouts  3.07 us

commit v1 on v0

--- a/solution.py
+++ b/solution.py
@@ -193,18 +193,11 @@
                     spot = orbit * (orbits + 1)
                     mm[row, pl.ds(spot, 1), :] += onsite_ref[row, pl.ds(orbit, 1), :]
 
-        def expand(orbit, inner):
-            for other in range(orbits):
-                spot = orbit * orbits + other
-                lines = [
-                    jnp.broadcast_to(mm[row, pl.ds(spot, 1), :], (8, width)) for row in range(4)
-                ]
-                top = jnp.where(sub8, lines[0], lines[1])
-                low = jnp.where(sub8, lines[2], lines[3])
-                blk[code * entries + spot] = jnp.concatenate([top, low], axis=0).astype(bf16)
-            return inner
-
-        lax.fori_loop(0, orbits, expand, 0)
+        for spot in range(entries):
+            lines = [jnp.broadcast_to(mm[row, spot : spot + 1, :], (8, width)) for row in range(4)]
+            top = jnp.where(sub8, lines[0], lines[1])
+            low = jnp.where(sub8, lines[2], lines[3])
+            blk[code * entries + spot] = jnp.concatenate([top, low], axis=0).astype(bf16)
         return carry
 
     lax.fori_loop(0, CODES, build, 0)
@@ -212,7 +205,7 @@
     tiles = []
     start = 0
     while start < orbits:
-        size = 4 if (orbits - start) % 3 else 3
+        size = 2 if orbits - start in (2, 4) else 3
         tiles.append((start, min(size, orbits - start)))
         start += size
 

time: 130 us -> 129 us (level)
  no operation moved by 1% of the time
where the time goes in v1:
time: 129 us
  Pallas kernels  121 us (94%)
  local copies, waits for them, and re-layouts  7.08 us (5%)
  other arithmetic  1.36 us (1%)
    pallas_call x1, Pallas kernels, body(): pl.pallas_call(functools.partial(kernel, orbits, groups), out_shape=jax.S...  121 us
    unnamed x8, local copies, waits for them, and re-layouts  3.07 us

profile of v1, /device:TPU:0, one launch (start us, length us, event | category | flops | bytes accessed | tf_op | source)
XLA Modules:
  0.0 129.0 jit_solution(13504050992817801790)
XLA Ops:
  0.0 0.0 copy-start.2
  0.0 0.0 copy-start.1
  0.0 0.0 copy-start
  0.0 0.7 copy-done.2
  0.7 0.7 broadcast_compare_fusion.2
  1.4 0.7 select_select_fusion.onsite_ref
  2.0 0.0 copy-done.1
  2.0 0.6 pad.9.weight_ref
  2.7 0.8 copy.10
  3.5 0.6 pad.8.gain_ref
  4.1 1.6 %copy.13 = bf16[128,4,128]{2,0,1:T(8,128)(2,1)} copy(bf16[128,4,128]{2,1,0:T(4,128)(2,1)} %param.8) | data formatting | bytes 262144 | tf_op args[1]
  5.7 0.0 copy-done
  5.7 0.9 copy.8
  6.6 120.5 %shard_map.73 = f32[52,16,128]{2,1,0:T(8,128)} custom-call(f32[52,16,128]{2,1,0:T(8,128)} %bitcast.20, bf16[4,128,128]{2,1,0:T(8,128)(2,1)} %bitcast.21, f32[128,128]{1,0:T(8,128)} %pad.8.gain_ref, bf16[176,128]{1,0:T(8,128)(2,1)} %pad.9.weight_ref, f32[4,13,128]{2,1,0:T(8,128)} %select_select_fusion.onsite_ref, s32[12,4,128]{2,1,0:T(4,128)} %near_ref.1), custom_call_target="tpu_custom_call" | custom-call | flops 276889600 | bytes 4194304 | tf_op jit(solution)/shard_map/pallas_call | solution.py:296
  127.1 1.9 %copy.11 = f32[4,4,13,4,128]{4,3,2,1,0:T(4,128)} copy(f32[4,4,13,4,128]{4,1,3,2,0:T(4,128)} %bitcast.19) | data formatting | bytes 851968 | tf_op jit(solution)/shard_map/transpose | solution.py:328
  (1 shorter events, 0.0 us)
Async XLA Ops:
  0.0 0.7 copy-start.2
  0.0 2.0 %copy-start.1 = (bf16[128,169]{0,1:T(8,128)(2,1)S(1)}, bf16[128,169]{0,1:T(8,128)(2,1)}, u32[]{:S(2)}) copy-start(bf16[128,169]{0,1:T(8,128)(2,1)} %param.10) | copy-start | bytes 129796
  0.0 5.7 %copy-start = (f32[16,13,4,128]{3,2,1,0:T(4,128)S(1)}, f32[16,13,4,128]{3,2,1,0:T(4,128)}, u32[]{:S(2)}) copy-start(f32[16,13,4,128]{3,2,1,0:T(4,128)} %param.7) | copy-start | bytes 1277956
